TPU v7x, 32 devices: a whole 2x2x4 slice. The times are simulated.
32 devices in a mesh: dp: 8 (over z, x), tensor: 4 (over y, core).
Axes of the slice: x: 2, y: 2, z: 4, core: 2. Of those that a mesh axis runs over, the one named last changes fastest.
Arguments:
- tokens: bfloat16 [10976, 1280], P(('dp', 'tensor')), may hold values from -6 to 6
- grad_out: bfloat16 [10976, 1280], P(('dp', 'tensor')), may hold values from -6 to 6
- adapter_index: int32 [2], replicated, may hold values from 0 to 7
- norm1_gain: bfloat16 [1280], replicated, may hold values from 0.099609375 to 1.8984375
- norm1_shift: bfloat16 [1280], replicated, may hold values from -2.5 to 2.5
- qkv_weight: bfloat16 [1280, 3, 1280], P(None, None, 'tensor'), may hold values from -0.15625 to 0.15625
- qkv_bias: bfloat16 [3, 1280], P(None, 'tensor'), may hold values from -2.5 to 2.5
- rel_pos_h: bfloat16 [27, 80], replicated, may hold values from -1.25 to 1.25
- rel_pos_w: bfloat16 [27, 80], replicated, may hold values from -1.25 to 1.25
- proj_weight: bfloat16 [1280, 1280], P('tensor'), may hold values from -0.625 to 0.625
- proj_bias: bfloat16 [1280], replicated, may hold values from -2.5 to 2.5
- norm2_gain: bfloat16 [1280], replicated, may hold values from 0.099609375 to 1.8984375
- norm2_shift: bfloat16 [1280], replicated, may hold values from -2.5 to 2.5
- lin1_weight: bfloat16 [1280, 5120], P(None, 'tensor'), may hold values from -0.15625 to 0.15625
- lin1_bias: bfloat16 [5120], P('tensor'), may hold values from -2.5 to 2.5
- lin2_weight: bfloat16 [5120, 1280], P('tensor'), may hold values from -0.078125 to 0.078125
- lin2_bias: bfloat16 [1280], replicated, may hold values from -2.5 to 2.5
- qkv_down: bfloat16 [8, 1280, 16], replicated, may hold values from -0.15625 to 0.15625
- qkv_up: bfloat16 [8, 16, 3, 1280], P(None, None, None, 'tensor'), may hold values from -1.5 to 1.5
- proj_down: bfloat16 [8, 1280, 16], P(None, 'tensor'), may hold values from -0.625 to 0.625
- proj_up: bfloat16 [8, 16, 1280], replicated, may hold values from -1.5 to 1.5
- lin1_down: bfloat16 [8, 1280, 16], replicated, may hold values from -0.15625 to 0.15625
- lin1_up: bfloat16 [8, 16, 5120], P(None, None, 'tensor'), may hold values from -1.5 to 1.5
- lin2_down: bfloat16 [8, 5120, 16], P(None, 'tensor'), may hold values from -0.078125 to 0.078125
- lin2_up: bfloat16 [8, 16, 1280], replicated, may hold values from -1.5 to 1.5
Outputs:
- output: bfloat16 [10976, 1280], P(('dp', 'tensor'))
- grad_tokens: bfloat16 [10976, 1280], P(('dp', 'tensor'))
- grad_qkv_down: float32 [8, 1280, 16], replicated
- grad_qkv_up: float32 [8, 16, 3, 1280], P(None, None, None, 'tensor')
- grad_proj_down: float32 [8, 1280, 16], P(None, 'tensor')
- grad_proj_up: float32 [8, 16, 1280], replicated
- grad_lin1_down: float32 [8, 1280, 16], replicated
- grad_lin1_up: float32 [8, 16, 5120], P(None, None, 'tensor')
- grad_lin2_down: float32 [8, 5120, 16], P(None, 'tensor')
- grad_lin2_up: float32 [8, 16, 1280], replicated
Inputs may be any that keep to these rules, and one draw needn't show every extreme that they name: `adapter_index`: one adapter for each image.
All inputs are finite; a program needn't handle non-finite values.
Results may differ from a plain program's by a relative error of at most 0.019.
Values may be sent and summed in bfloat16 or wider, within the bound.
A program may use at most 256 MiB of HBM per device.

v0:
```python
import jax
import jax.numpy as jnp
from jax import lax
from jax.sharding import PartitionSpec as P

HEAD_DIM = 80
WIN = 14
SIDE = 64
RANK = 16
ADAPTERS = 8
WIN_DEV = 7
GROUP = 4
GRID = 5
HIGH = lax.Precision.HIGHEST
ADAPT = 0.5
EPS = 1e-06


def fast_dot(first_op, second_op):
    return jnp.dot(first_op, second_op, preferred_element_type=jnp.float32)


def trans_dot(first_op, second_op):
    return lax.dot_general(
        first_op, second_op, (((1,), (1,)), ((), ())), preferred_element_type=jnp.float32
    )


def exact_dot(first_op, second_op):
    return jnp.dot(first_op, second_op.astype(jnp.float32), precision=HIGH)


def cross_dot(first_op, second_op):
    return lax.dot_general(
        first_op.astype(jnp.float32),
        second_op.astype(jnp.float32),
        (((0,), (0,)), ((), ())),
        precision=HIGH,
    )


def window_mask(first_slot, count_all):
    position = jnp.arange(count_all, dtype=jnp.int32)
    slot_index = first_slot + position // (WIN * WIN)
    within = position % (WIN * WIN)
    image_row = slot_index // GRID * WIN + within // WIN
    image_col = slot_index % GRID * WIN + within % WIN
    inside = (slot_index < GRID * GRID) & (image_row < SIDE) & (image_col < SIDE)
    return jnp.where(inside, 1.0, 0.0).astype(jnp.float32)[:, None]


def offset_table(position_table):
    offsets = (jnp.arange(WIN)[:, None] - jnp.arange(WIN)[None, :] + WIN - 1).reshape(-1)
    one_hot = (offsets[:, None] == jnp.arange(2 * WIN - 1)[None, :]).astype(jnp.float32)
    return exact_dot(one_hot, position_table).reshape(WIN, WIN, -1).astype(jnp.bfloat16)


def norm_parts(values):
    row_mean = jnp.mean(values, axis=-1, keepdims=True)
    centered = values - row_mean
    inv_std = lax.rsqrt(jnp.mean(centered * centered, axis=-1, keepdims=True) + EPS)
    return (centered * inv_std, inv_std)


def norm_back(grad_in, normalized, inv_std, norm_gain):
    scaled = grad_in * norm_gain
    return inv_std * (
        scaled
        - jnp.mean(scaled, axis=-1, keepdims=True)
        - normalized * jnp.mean(scaled * normalized, axis=-1, keepdims=True)
    )


def window_scores(queries, key_win, table_h, table_w):
    win_count, head_count = (queries.shape[0], queries.shape[1])
    tokens_win = WIN * WIN
    base_scores = jnp.einsum(
        "nhqc,nhkc->nhqk",
        queries.reshape(win_count, head_count, tokens_win, -1),
        key_win.reshape(win_count, head_count, tokens_win, -1),
        preferred_element_type=jnp.float32,
    ) * HEAD_DIM ** (-0.5)
    rel_rows = jnp.einsum("nhabc,akc->nhabk", queries, table_h, preferred_element_type=jnp.float32)
    rel_cols = jnp.einsum("nhabc,bkc->nhabk", queries, table_w, preferred_element_type=jnp.float32)
    scores = (
        base_scores.reshape(win_count, head_count, WIN, WIN, WIN, WIN)
        + rel_rows[:, :, :, :, :, None]
        + rel_cols[:, :, :, :, None, :]
    )
    return scores.reshape(win_count, head_count, tokens_win, tokens_win)


def attention_back(queries, key_win, value_win, log_total, grad_att, table_h, table_w):
    win_count, head_count = (queries.shape[0], queries.shape[1])
    tokens_win = WIN * WIN
    probs = jnp.exp(window_scores(queries, key_win, table_h, table_w) - log_total)
    grad_rows = grad_att.reshape(win_count, head_count, tokens_win, -1)
    dprob = jnp.einsum(
        "nhqc,nhkc->nhqk",
        grad_rows,
        value_win.reshape(win_count, head_count, tokens_win, -1),
        preferred_element_type=jnp.float32,
    )
    dvalues = jnp.einsum(
        "nhqk,nhqc->nhkc", probs.astype(jnp.bfloat16), grad_rows, preferred_element_type=jnp.float32
    )
    inner_sum = jnp.sum(probs * dprob, axis=-1, keepdims=True)
    dscore = (probs * (dprob - inner_sum)).astype(jnp.bfloat16)
    dqueries = jnp.einsum(
        "nhqk,nhkc->nhqc",
        dscore,
        key_win.reshape(win_count, head_count, tokens_win, -1),
        preferred_element_type=jnp.float32,
    ) * HEAD_DIM ** (-0.5)
    dkeys = jnp.einsum(
        "nhqk,nhqc->nhkc",
        dscore,
        queries.reshape(win_count, head_count, tokens_win, -1),
        preferred_element_type=jnp.float32,
    ) * HEAD_DIM ** (-0.5)
    dscore_six = dscore.astype(jnp.float32).reshape(win_count, head_count, WIN, WIN, WIN, WIN)
    from_rows = jnp.einsum(
        "nhabk,akc->nhabc", jnp.sum(dscore_six, axis=5), table_h.astype(jnp.float32), precision=HIGH
    )
    from_cols = jnp.einsum(
        "nhabk,bkc->nhabc", jnp.sum(dscore_six, axis=4), table_w.astype(jnp.float32), precision=HIGH
    )
    dqueries = dqueries.reshape(queries.shape) + from_rows + from_cols
    return (
        dqueries.astype(jnp.bfloat16),
        dkeys.reshape(queries.shape).astype(jnp.bfloat16),
        dvalues.reshape(queries.shape).astype(jnp.bfloat16),
    )


def on_device(
    tokens,
    grad_out,
    adapter_index,
    norm1_gain,
    norm1_shift,
    qkv_weight,
    qkv_bias,
    rel_pos_h,
    rel_pos_w,
    proj_weight,
    proj_bias,
    norm2_gain,
    norm2_shift,
    lin1_weight,
    lin1_bias,
    lin2_weight,
    lin2_bias,
    qkv_down,
    qkv_up,
    proj_down,
    proj_up,
    lin1_down,
    lin1_up,
    lin2_down,
    lin2_up,
):
    tensor_size = lax.axis_size("tensor")
    row_count = tokens.shape[0]
    full_rows = row_count * tensor_size
    dp_place = lax.axis_index("dp")
    tensor_place = lax.axis_index("tensor")
    valid_full = window_mask(dp_place % GROUP * WIN_DEV, full_rows)
    valid_local = lax.dynamic_slice_in_dim(valid_full, tensor_place * row_count, row_count, 0)
    image_place = dp_place // GROUP
    pick = jnp.sum(jnp.where(jnp.arange(adapter_index.shape[0]) == image_place, adapter_index, 0))
    slot_hot = jnp.where(jnp.arange(ADAPTERS) == pick, 1.0, 0.0).astype(jnp.float32)

    def select(table_all):
        return lax.dynamic_index_in_dim(table_all, pick, 0, keepdims=False)

    def into_slot(term):
        return slot_hot.reshape((-1,) + (1,) * term.ndim) * term[None]

    head_local = qkv_weight.shape[2] // HEAD_DIM
    width_local = qkv_weight.shape[2]

    def to_windows(values):
        return values.reshape(-1, WIN, WIN, head_local, HEAD_DIM).transpose(0, 3, 1, 2, 4)

    def from_windows(values):
        return values.transpose(0, 2, 3, 1, 4).reshape(full_rows, -1)

    gain_one = norm1_gain.astype(jnp.float32)
    gain_two = norm2_gain.astype(jnp.float32)
    table_h = offset_table(rel_pos_h)
    table_w = offset_table(rel_pos_w)
    a_qkv = select(qkv_down)
    b_qkv = select(qkv_up).reshape(RANK, -1)
    a_proj = select(proj_down)
    b_proj = select(proj_up)
    a_lin1 = select(lin1_down)
    b_lin2 = select(lin2_up)
    qkv_flat = qkv_weight.reshape(qkv_weight.shape[0], -1)
    x_local = tokens.astype(jnp.float32)
    normal_one, inv_one = norm_parts(x_local)
    xn1_local = (valid_local * (normal_one * gain_one + norm1_shift.astype(jnp.float32))).astype(
        jnp.bfloat16
    )
    xn1 = lax.all_gather(xn1_local, "tensor", axis=0, tiled=True)
    down_q = fast_dot(xn1, a_qkv)
    qkv = (
        fast_dot(xn1, qkv_flat)
        + qkv_bias.astype(jnp.float32).reshape(-1)
        + ADAPT * exact_dot(down_q, b_qkv)
    )
    qkv = qkv.astype(jnp.bfloat16).reshape(full_rows, 3, width_local)
    queries = to_windows(qkv[:, 0])
    key_win = to_windows(qkv[:, 1])
    value_win = to_windows(qkv[:, 2])
    win_count = queries.shape[0]
    tokens_win = WIN * WIN
    scores = window_scores(queries, key_win, table_h, table_w)
    row_max = jnp.max(scores, axis=-1, keepdims=True)
    exponent = jnp.exp(scores - row_max)
    row_total = jnp.sum(exponent, axis=-1, keepdims=True)
    log_total = row_max + jnp.log(row_total)
    probs = exponent / row_total
    attended = jnp.einsum(
        "nhqk,nhkc->nhqc",
        probs.astype(jnp.bfloat16),
        value_win.reshape(win_count, head_local, tokens_win, -1),
        preferred_element_type=jnp.float32,
    )
    att = from_windows(attended.reshape(queries.shape)).astype(jnp.bfloat16)
    down_p = fast_dot(att, a_proj)
    down_part = down_p
    branch_a = lax.psum_scatter(
        (fast_dot(att, proj_weight) + ADAPT * exact_dot(down_part, b_proj)).astype(jnp.bfloat16),
        "tensor",
        scatter_dimension=0,
        tiled=True,
    ).astype(jnp.float32)
    middle = x_local + valid_local * (branch_a + proj_bias.astype(jnp.float32))
    normal_two, inv_two = norm_parts(middle)
    xn2_local = (normal_two * gain_two + norm2_shift.astype(jnp.float32)).astype(jnp.bfloat16)
    xn2 = lax.all_gather(xn2_local, "tensor", axis=0, tiled=True)
    w_lin1, c_lin1, b_lin1, a_lin2, w_lin2 = (
        lin1_weight,
        lin1_bias,
        select(lin1_up),
        select(lin2_down),
        lin2_weight,
    )
    down_1 = fast_dot(xn2, a_lin1)
    hidden_pre = (
        fast_dot(xn2, w_lin1) + c_lin1.astype(jnp.float32) + ADAPT * exact_dot(down_1, b_lin1)
    )
    gelu_value, gelu_grad = jax.vjp(
        lambda values: jax.nn.gelu(values, approximate=False), hidden_pre
    )
    hidden_act = gelu_value.astype(jnp.bfloat16)
    down_2 = fast_dot(hidden_act, a_lin2)
    down_part = down_2
    branch_m = lax.psum_scatter(
        (fast_dot(hidden_act, w_lin2) + ADAPT * exact_dot(down_part, b_lin2)).astype(jnp.bfloat16),
        "tensor",
        scatter_dimension=0,
        tiled=True,
    ).astype(jnp.float32)
    output = (middle + valid_local * (branch_m + lin2_bias.astype(jnp.float32))).astype(
        jnp.bfloat16
    )
    dout_f = grad_out.astype(jnp.float32)
    dy2_local = (valid_local * dout_f).astype(jnp.bfloat16)
    dy2 = lax.all_gather(dy2_local, "tensor", axis=0, tiled=True)
    up2 = trans_dot(dy2, b_lin2)
    dact = trans_dot(dy2, w_lin2) + ADAPT * exact_dot(up2, a_lin2.T)
    dpre = gelu_grad(dact)[0].astype(jnp.bfloat16)
    up1 = trans_dot(dpre, b_lin1)
    grad_lin2_up_t = ADAPT * cross_dot(down_2, dy2)
    grad_lin2_down_t = ADAPT * cross_dot(hidden_act, up2)
    grad_lin1_up_t = ADAPT * cross_dot(down_1, dpre)
    grad_lin1_down_t = ADAPT * cross_dot(xn2, up1)
    up_part = up1
    dxn2 = lax.psum_scatter(
        (trans_dot(dpre, w_lin1) + ADAPT * exact_dot(up_part, a_lin1.T)).astype(jnp.bfloat16),
        "tensor",
        scatter_dimension=0,
        tiled=True,
    ).astype(jnp.float32)
    dmiddle = dout_f + norm_back(dxn2, normal_two, inv_two, gain_two)
    dya_local = (valid_local * dmiddle).astype(jnp.bfloat16)
    dya = lax.all_gather(dya_local, "tensor", axis=0, tiled=True)
    upp = trans_dot(dya, b_proj)
    datt = (trans_dot(dya, proj_weight) + ADAPT * exact_dot(upp, a_proj.T)).astype(jnp.bfloat16)
    grad_proj_up_t = ADAPT * cross_dot(down_p, dya)
    grad_proj_down_t = ADAPT * cross_dot(att, upp)
    dqueries, dkeys, dvalues = attention_back(
        queries, key_win, value_win, log_total, to_windows(datt), table_h, table_w
    )
    dqkv = jnp.stack(
        [from_windows(dqueries), from_windows(dkeys), from_windows(dvalues)], axis=1
    ).reshape(full_rows, -1)
    upq = trans_dot(dqkv, b_qkv)
    grad_qkv_up_t = (ADAPT * cross_dot(down_q, dqkv)).reshape(RANK, 3, -1)
    grad_qkv_down_t = ADAPT * cross_dot(xn1, upq)
    up_part = upq
    dxn1 = lax.psum_scatter(
        (trans_dot(dqkv, qkv_flat) + ADAPT * exact_dot(up_part, a_qkv.T)).astype(jnp.bfloat16),
        "tensor",
        scatter_dimension=0,
        tiled=True,
    ).astype(jnp.float32)
    grad_tokens = (dmiddle + norm_back(valid_local * dxn1, normal_one, inv_one, gain_one)).astype(
        jnp.bfloat16
    )
    grad_qkv_up, grad_proj_down, grad_lin1_up, grad_lin2_down = lax.psum(
        (
            into_slot(grad_qkv_up_t),
            into_slot(grad_proj_down_t),
            into_slot(grad_lin1_up_t),
            into_slot(grad_lin2_down_t),
        ),
        "dp",
    )
    grad_qkv_down, grad_proj_up, grad_lin1_down, grad_lin2_up = lax.psum(
        (
            into_slot(grad_qkv_down_t),
            into_slot(grad_proj_up_t),
            into_slot(grad_lin1_down_t),
            into_slot(grad_lin2_up_t),
        ),
        ("dp", "tensor"),
    )
    return (
        output,
        grad_tokens,
        grad_qkv_down,
        grad_qkv_up,
        grad_proj_down,
        grad_proj_up,
        grad_lin1_down,
        grad_lin1_up,
        grad_lin2_down,
        grad_lin2_up,
    )


def solution(mesh):
    placed = (
        P(("dp", "tensor"), None),
        P(("dp", "tensor"), None),
        P(),
        P(),
        P(),
        P(None, None, "tensor"),
        P(None, "tensor"),
        P(),
        P(),
        P("tensor", None),
        P(),
        P(),
        P(),
        P(None, "tensor"),
        P("tensor"),
        P("tensor", None),
        P(),
        P(),
        P(None, None, None, "tensor"),
        P(None, "tensor", None),
        P(),
        P(),
        P(None, None, "tensor"),
        P(None, "tensor", None),
        P(),
    )
    return jax.shard_map(
        on_device,
        mesh=mesh,
        in_specs=placed,
        out_specs=(
            P(("dp", "tensor"), None),
            P(("dp", "tensor"), None),
            P(),
            P(None, None, None, "tensor"),
            P(None, "tensor", None),
            P(),
            P(),
            P(None, None, "tensor"),
            P(None, "tensor", None),
            P(),
        ),
        check_vma=False,
    )
```

profile of v0, /device:TPU:0, one launch (start us, length us, event | category | flops | bytes accessed | tf_op | source)
XLA Modules:
  0.0 929.5 jit_solution(8334608292282891529)
XLA Ops:
  19.2 28.9 %all-gather.9.cloned.1.call-done = bf16[4,343,1280]{2,1,0:T(8,128)(2,1)} async-done(((bf16[1,343,1280]{2,1,0:T(8,128)(2,1)}), bf16[4,343,1280]{2,1,0:T(8,128)(2,1)}) %all-gather.9.cloned.1.call-update) | async-done | bytes 3512336 | tf_op jit(solution)/shard_map/all_gather | solution.py:205
  100.1 6.8 convolution_bitcast_fusion.2
  112.7 6.8 convolution_bitcast_fusion.1
  125.8 16.1 %add.258 = f32[7,4,14,14,14,14]{5,4,3,2,1,0:T(8,128)} broadcast(f32[7,4,14,14,14]{4,3,2,1,0:T(8,128)} %copy.105), dimensions={0,1,2,3,5} | broadcast | bytes 4609920 | tf_op jit(solution)/shard_map/add | solution.py:86
  141.9 26.9 %add.259 = f32[7,4,196,196]{3,2,1,0:T(8,128)} reshape(f32[7,4,14,14,14,14]{5,4,3,2,1,0:T(8,128)} %add.258) | data formatting | bytes 8605184 | tf_op jit(solution)/shard_map/add | solution.py:86
  168.8 6.8 copy.106
  175.6 16.6 %add.255 = f32[7,4,14,14,14,14]{5,4,3,2,1,0:T(8,128)} broadcast(f32[7,4,14,14,14]{4,3,2,1,0:T(8,128)} %copy.101), dimensions={0,1,2,3,4} | broadcast | bytes 4609920 | tf_op jit(solution)/shard_map/add | solution.py:86
  192.2 26.9 %add.256 = f32[7,4,196,196]{3,2,1,0:T(8,128)} reshape(f32[7,4,14,14,14,14]{5,4,3,2,1,0:T(8,128)} %add.255) | data formatting | bytes 8605184 | tf_op jit(solution)/shard_map/add | solution.py:86
  219.1 6.5 copy.102
  254.6 35.5 %fusion = bf16[344,1280]{1,0:T(8,128)(2,1)} fusion(bf16[1372,1280]{1,0:T(8,128)(2,1)} %fusion.13), kind=kCustom, calls=%all-reduce-scatter | all-reduce-scatter fusion | flops 1761281 | bytes 4393472
  306.8 33.4 %all-gather.13.cloned.1.call-done = bf16[4,343,1280]{2,1,0:T(8,128)(2,1)} async-done(((bf16[1,343,1280]{2,1,0:T(8,128)(2,1)}), bf16[4,343,1280]{2,1,0:T(8,128)(2,1)}) %all-gather.13.cloned.1.call-update) | async-done | bytes 3512336 | tf_op jit(solution)/shard_map/all_gather | solution.py:271
  348.1 9.0 fusion.152
  357.2 15.9 %all-gather.11.cloned.1.call-done = bf16[4,343,1280]{2,1,0:T(8,128)(2,1)} async-done(((bf16[1,343,1280]{2,1,0:T(8,128)(2,1)}), bf16[4,343,1280]{2,1,0:T(8,128)(2,1)}) %all-gather.11.cloned.1.call-update) | async-done | bytes 3512336 | tf_op jit(solution)/shard_map/all_gather | solution.py:242
  386.0 22.5 %multiply_convert_fusion = (bf16[1372,1280]{1,0:T(8,128)(2,1)}, f32[1372,1280]{1,0:T(8,128)S(1)}, f32[1372,1280]{1,0:T(8,128)}) fusion(f32[1372,1280]{1,0:T(8,128)S(1)} %convolution_add_fusion, f32[1372,16]{0,1:T(8,128)S(1)} %fusion.81, bf16[8,16,1280]{2,1,0:T(8,128)(2,1)} %param.47, s32[]{:T(128)S(6)} %select_n.86), kind=kOutput, calls=%fused_computation.21 | convolution fusion | flops 454845440 | bytes 24715012 | tf_op jit(solution)/shard_map/dot_general | solution.py:30
  408.5 9.7 %add_convert_fusion = bf16[1372,1280]{1,0:T(8,128)(2,1)S(1)} fusion(f32[1372,1280]{1,0:T(8,128)S(1)} %get-tuple-element.31, f32[1372,1280]{1,0:T(8,128)S(1)} %bitcast.198, f32[1372,16]{0,1:T(8,128)S(1)} %fusion.71, f32[1372,1280]{1,0:T(8,128)} %get-tuple-element.47, bf16[8,1280,16]{1,2,0:T(8,128)(2,1)} %param.48, s32[]{:T(128)S(6)} %select_n.86), kind=kOutput, calls=%fused_computation.20 | convolution fusion | flops 365281280 | bytes 24735492 | tf_op jit(solution)/shard_map/dot_general | solution.py:30
  430.9 35.2 %fusion.2 = bf16[344,1280]{1,0:T(8,128)(2,1)} fusion(bf16[1372,1280]{1,0:T(8,128)(2,1)} %fusion.11), kind=kCustom, calls=%all-reduce-scatter.2 | all-reduce-scatter fusion | flops 1761281 | bytes 4393472
  469.0 6.7 concatenate.2
  502.1 6.5 fusion.12
  508.5 9.3 all-gather.15.cloned.1.call-done
  588.3 26.1 %reshape.202 = f32[7,4,14,14,14,14]{5,4,3,2,1,0:T(8,128)} reshape(f32[7,4,196,196]{3,2,1,0:T(8,128)} %copy.117) | data formatting | bytes 8605184 | tf_op jit(solution)/shard_map/reshape | solution.py:121
  614.4 19.9 %fusion.144 = (f32[7,4,14,14,14]{4,3,2,1,0:T(8,128)}, f32[7,4,14,14,14]{4,3,2,1,0:T(8,128)}) fusion(f32[7,4,14,14,14,14]{5,4,3,2,1,0:T(8,128)} %reshape.202), kind=kLoop, calls=%fused_computation.232 | loop fusion | flops 1997632 | bytes 4917248 | tf_op jit(solution)/shard_map/reduce_sum | solution.py:123
  678.7 68.8 %fusion.145 = (bf16[344,1280]{1,0:T(8,128)(2,1)}, bf16[344,1280]{1,0:T(8,128)(2,1)}) fusion(bf16[1372,1280]{1,0:T(8,128)(2,1)} %fusion.12, bf16[1372,1280]{1,0:T(8,128)(2,1)} %fusion.10), kind=kCustom, calls=%all-reduce-scatter.4 | all-reduce-scatter fusion | flops 3522561 | bytes 8786432
  773.5 31.3 %all-reduce.14.cloned.1.call-done = (f32[8,1280,16]{1,2,0:T(8,128)}, f32[8,16,1280]{2,1,0:T(8,128)}, f32[8,1280,16]{1,2,0:T(8,128)}, f32[8,16,1280]{2,1,0:T(8,128)}) async-done(((f32[8,1280,16]{1,2,0:T(8,128)}, f32[8,16,1280]{2,1,0:T(8,128)}, f32[8,1280,16]{1,2,0:T(8,128)}, f32[8,16,1280]{2,1,0:T(8,128)}), (f32[8,1280,16]{1,2,0:T(8,128)}, f32[8,16,1280]{2,1,0:T(8,128)}, f32[8,1280,16]{1,2,0:T(8,128)}, ...) | async-done | bytes 2621456 | tf_op jit(solution)/shard_map/psum | solution.py:322
  804.8 107.7 %all-reduce.16.cloned.1.call-done = (f32[8,16,3,320]{3,1,2,0:T(8,128)}, f32[8,320,16]{1,2,0:T(8,128)}, f32[8,16,1280]{2,1,0:T(8,128)}, f32[8,1280,16]{1,2,0:T(8,128)}) async-done(((f32[8,16,3,320]{3,1,2,0:T(8,128)}, f32[8,320,16]{1,2,0:T(8,128)}, f32[8,16,1280]{2,1,0:T(8,128)}, f32[8,1280,16]{1,2,0:T(8,128)}), (f32[8,16,3,320]{3,1,2,0:T(8,128)}, f32[8,320,16]{1,2,0:T(8,128)}, f32[8,16,1280]{2,1,0:T(8,128)}, ...) | async-done | bytes 1966096 | tf_op jit(solution)/shard_map/psum | solution.py:313
  (300 shorter events, 331.8 us)
Async XLA Ops:
  7.2 373.8 %copy-start = (bf16[1280,1280]{1,0:T(8,128)(2,1)S(1)}, bf16[1280,1280]{1,0:T(8,128)(2,1)}, u32[]{:S(2)}) copy-start(bf16[1280,1280]{1,0:T(8,128)(2,1)} %param.38) | copy-start | bytes 9830404
  7.2 40.8 %all-gather.9.cloned.1.call-start = ((), (), s32[]{:S(2)}) async-start(), calls=%async_computation | async-start | bytes 4403200 | tf_op jit(solution)/shard_map/all_gather | solution.py:205
  14.5 325.7 %all-gather.13.cloned.1.call-start = ((), (), s32[]{:S(2)}) async-start(), calls=%async_computation.2 | async-start | bytes 4403200 | tf_op jit(solution)/shard_map/all_gather | solution.py:271
  18.3 43.4 %copy-start.45 = (bf16[16,960]{1,0:T(8,128)(2,1)}, bf16[16,960]{1,0:T(8,128)(2,1)S(1)}, u32[]{:S(2)}) copy-start(bf16[16,960]{1,0:T(8,128)(2,1)S(1)} %reshape.189) | copy-start | bytes 92164
  18.7 93.9 %copy-start.40 = (bf16[14,14,80,1,1]{2,1,0,3,4:T(8,128)(2,1)}, bf16[14,14,80,1,1]{2,1,0,3,4:T(8,128)(2,1)S(1)}, u32[]{:S(2)}) copy-start(bf16[14,14,80,1,1]{2,1,0,3,4:T(8,128)(2,1)S(1)} %reshape.212) | copy-start | bytes 94084
  19.2 80.9 %copy-start.42 = (bf16[14,14,80,1,1]{2,1,0,3,4:T(8,128)(2,1)}, bf16[14,14,80,1,1]{2,1,0,3,4:T(8,128)(2,1)S(1)}, u32[]{:S(2)}) copy-start(bf16[14,14,80,1,1]{2,1,0,3,4:T(8,128)(2,1)S(1)} %reshape.211) | copy-start | bytes 94084
  254.6 37.5 %copy-start.53 = (bf16[1280]{0:T(1024)(128)(2,1)S(1)}, bf16[1280]{0:T(1024)(128)(2,1)}, u32[]{:S(2)}) copy-start(bf16[1280]{0:T(1024)(128)(2,1)} %param.35) | copy-start | bytes 7684
  254.6 37.6 %copy-start.54 = (bf16[1280]{0:T(1024)(128)(2,1)S(1)}, bf16[1280]{0:T(1024)(128)(2,1)}, u32[]{:S(2)}) copy-start(bf16[1280]{0:T(1024)(128)(2,1)} %param.36) | copy-start | bytes 7684
  254.6 37.6 %copy-start.55 = (bf16[1280]{0:T(1024)(128)(2,1)S(1)}, bf16[1280]{0:T(1024)(128)(2,1)}, u32[]{:S(2)}) copy-start(bf16[1280]{0:T(1024)(128)(2,1)} %param.37) | copy-start | bytes 7684
  254.6 37.6 %copy-start.59 = (u32[32]{0:T(128)S(1)}, u32[32]{0:T(128)}, u32[]{:S(2)}) copy-start(u32[32]{0:T(128)} %constant.209) | copy-start | bytes 388
  290.8 2.6 collective-permute-start
  306.0 67.1 %all-gather.11.cloned.1.call-start = ((), (), s32[]{:S(2)}) async-start(), calls=%async_computation.1 | async-start | bytes 4403200 | tf_op jit(solution)/shard_map/all_gather | solution.py:242
  306.7 211.1 %all-gather.15.cloned.1.call-start = ((), (), s32[]{:S(2)}) async-start(), calls=%async_computation.3 | async-start | bytes 4403200 | tf_op jit(solution)/shard_map/all_gather | solution.py:289
  348.1 60.4 %copy-start.37 = (f32[1372,16]{0,1:T(8,128)}, f32[1372,16]{0,1:T(8,128)S(1)}, u32[]{:S(2)}) copy-start(f32[1372,16]{0,1:T(8,128)S(1)} %fusion.71) | copy-start | bytes 263428
  381.1 27.4 %slice-start.2 = ((s8[7045120]{0:T(1024)(128)(4,1)}), s8[4194304]{0:T(1024)(128)(4,1)S(1)}, s32[]{:S(2)}) async-start(s8[7045120]{0:T(1024)(128)(4,1)} %bitcast.197), calls=%async_computation.8 | async-start | bytes 8388608
  386.0 22.5 %slice-start.3 = ((s8[7045120]{0:T(1024)(128)(4,1)}), s8[2850816]{0:T(1024)(128)(4,1)S(1)}, s32[]{:S(2)}) async-start(s8[7045120]{0:T(1024)(128)(4,1)} %bitcast.197), calls=%async_computation.9 | async-start | bytes 5701632
  466.8 2.2 collective-permute-start.2
  483.1 321.8 %all-reduce.14.cloned.1.call-start = ((), (), s32[]{:S(2)}) async-start(), calls=%async_computation.4 | async-start | bytes 5242880 | tf_op jit(solution)/shard_map/psum | solution.py:322
  614.4 19.9 %copy-start.41 = (bf16[14,14,80,1,1]{2,1,0,3,4:T(8,128)(2,1)S(1)}, bf16[14,14,80,1,1]{2,1,0,3,4:T(8,128)(2,1)}, u32[]{:S(2)}) copy-start(bf16[14,14,80,1,1]{2,1,0,3,4:T(8,128)(2,1)} %copy-done.40) | copy-start | bytes 94084
  666.3 246.2 %all-reduce.16.cloned.1.call-start = ((), (), s32[]{:S(2)}) async-start(), calls=%async_computation.5 | async-start | bytes 4194304 | tf_op jit(solution)/shard_map/psum | solution.py:313
  678.7 74.8 %copy-start.57 = (bf16[1280]{0:T(1024)(128)(2,1)S(1)}, bf16[1280]{0:T(1024)(128)(2,1)}, u32[]{:S(2)}) copy-start(bf16[1280]{0:T(1024)(128)(2,1)} %param.41) | copy-start | bytes 7684
  747.5 18.1 %copy-start.52 = (f32[343]{0:T(512)S(1)}, f32[343]{0:T(512)}, u32[]{:S(2)}) copy-start(f32[343]{0:T(512)} %copy-done.51) | copy-start | bytes 4120
  748.3 5.2 collective-permute-start.3
  750.3 9.2 collective-permute-start.1
  (54 other events, 293.1 us)
Sparse Core Ops, SparseCore 0:
  14.7 33.3 all-gather.8
  306.1 34.0 all-gather.12
  342.4 30.6 all-gather.10
  483.2 34.5 all-gather.14
  666.4 138.3 all-reduce.13
  810.3 102.1 all-reduce.15
where the time goes:
time: 941 us; the launch traced here: 930 us
  local copies, waits for them, and re-layouts  291 us (31%)
  waiting for transfers between devices  228 us (24%)
  matrix products  184 us (20%)
  blocking collectives  140 us (15%)
  other arithmetic  61.4 us (7%)
  between operations  17.9 us (2%)
    unnamed x3, blocking collectives  140 us
    psum x1, waiting for transfers between devices, on_device(): lax.psum((into_slot(grad_qkv_up_t), into_slot(grad_proj_down_t), into_slo...  108 us
    add x6, local copies, waits for them, and re-layouts, window_scores(): base_scores.reshape(win_count, head_count, WIN, WIN, WIN, WIN)  99.8 us
    unnamed x160, local copies, waits for them, and re-layouts  66.6 us
    dot_general x10, matrix products, exact_dot(): return jnp.dot(first_op, second_op.astype(jnp.float32), precision=HIGH)  62.1 us
    all_gather x1, waiting for transfers between devices, on_device(): dy2 = lax.all_gather(dy2_local, 'tensor', axis=0, tiled=True)  33.4 us
    reshape x2, local copies, waits for them, and re-layouts, attention_back(): dscore.astype(jnp.float32)  31.3 us
    psum x1, waiting for transfers between devices, on_device(): lax.psum((into_slot(grad_qkv_down_t), into_slot(grad_proj_up_t), into_slo...  31.3 us
  transfers between devices with their start and end apart: 10, of which 7 were waited for; matrix products, arithmetic and copies ran while one was open for 16% of the time, Pallas kernels for 0%

commit v1 on v0

--- a/solution.py
+++ b/solution.py
@@ -14,6 +14,12 @@
 HIGH = lax.Precision.HIGHEST
 ADAPT = 0.5
 EPS = 1e-06
+
+
+def in_order(tiles, dim):
+    shape = list(tiles.shape[1:])
+    shape[dim] *= tiles.shape[0]
+    return jnp.moveaxis(tiles, 0, dim).reshape(shape)
 
 
 def fast_dot(first_op, second_op):
@@ -202,7 +208,14 @@
     xn1_local = (valid_local * (normal_one * gain_one + norm1_shift.astype(jnp.float32))).astype(
         jnp.bfloat16
     )
-    xn1 = lax.all_gather(xn1_local, "tensor", axis=0, tiled=True)
+    length = lax.axis_size("tensor")
+    forward = [(i, (i + 1) % length) for i in range(length)]
+    blocks = [xn1_local]
+    while len(blocks) < length:
+        blocks.append(lax.ppermute(blocks[-1], "tensor", forward))
+    index = lax.axis_index("tensor")
+    blocks = jnp.stack(blocks)[(index - jnp.arange(length)) % length]
+    xn1 = in_order(blocks, 0)
     down_q = fast_dot(xn1, a_qkv)
     qkv = (
         fast_dot(xn1, qkv_flat)

time: 941 us -> 950 us (level)
    ppermute x0 -> x3, waiting for transfers between devices: none -> 31.9 us  [on_device(): blocks.append(lax.ppermute(blocks[-1], 'tensor', forward))]
    all_gather x1 -> x0, waiting for transfers between devices: 28.9 us -> none  [on_device(): xn1 = lax.all_gather(xn1_local, 'tensor', axis=0, tiled=True)]
    unnamed x160 -> x159, local copies, waits for them, and re-layouts: 66.6 us -> 61.7 us
  transfers between devices with their start and end apart: 10 -> 12, of which waited for: 7 -> 9; matrix products, arithmetic and copies ran while one was open for 16% -> 16% of each run, Pallas kernels for 0% -> 0%
where the time goes in v1:
time: 950 us; the launch traced here: 942 us
  local copies, waits for them, and re-layouts  295 us (31%)
  waiting for transfers between devices  231 us (24%)
  matrix products  184 us (19%)
  blocking collectives  140 us (15%)
  other arithmetic  66 us (7%)
  between operations  17.5 us (2%)
    unnamed x3, blocking collectives  140 us
    psum x1, waiting for transfers between devices, on_device(): lax.psum((into_slot(grad_qkv_up_t), into_slot(grad_proj_down_t), into_slo...  108 us
    add x6, local copies, waits for them, and re-layouts, window_scores(): base_scores.reshape(win_count, head_count, WIN, WIN, WIN, WIN)  99.7 us
    dot_general x10, matrix products, exact_dot(): return jnp.dot(first_op, second_op.astype(jnp.float32), precision=HIGH)  61.7 us
    unnamed x159, local copies, waits for them, and re-layouts  61.7 us
    all_gather x1, waiting for transfers between devices, on_device(): dy2 = lax.all_gather(dy2_local, 'tensor', axis=0, tiled=True)  33.8 us
    ppermute x3, waiting for transfers between devices, on_device(): blocks.append(lax.ppermute(blocks[-1], 'tensor', forward))  31.9 us
    reshape x2, local copies, waits for them, and re-layouts, attention_back(): dscore.astype(jnp.float32)  31.3 us
  transfers between devices with their start and end apart: 12, of which 9 were waited for; matrix products, arithmetic and copies ran while one was open for 16% of the time, Pallas kernels for 0%

profile of v1, /device:TPU:0, one launch (start us, length us, event | category | flops | bytes accessed | tf_op | source)
XLA Modules:
  0.0 942.2 jit_solution(11182303753271264866)
XLA Ops:
  14.1 12.7 %collective-permute-done = bf16[343,1280]{1,0:T(8,128)(2,1)} collective-permute-done((bf16[343,1280]{1,0:T(8,128)(2,1)S(1)}, bf16[343,1280]{1,0:T(8,128)(2,1)}, u32[]{:S(2)}, u32[]{:S(2)}) %collective-permute-start) | collective-permute-done | bytes 878112 | tf_op jit(solution)/shard_map/ppermute | solution.py:215
  31.0 8.6 collective-permute-done.1
  41.8 10.6 %collective-permute-done.2 = bf16[343,1280]{1,0:T(8,128)(2,1)} collective-permute-done((bf16[343,1280]{1,0:T(8,128)(2,1)}, bf16[343,1280]{1,0:T(8,128)(2,1)}, u32[]{:S(2)}, u32[]{:S(2)}) %collective-permute-start.2) | collective-permute-done | bytes 878112 | tf_op jit(solution)/shard_map/ppermute | solution.py:215
  112.5 6.8 convolution_bitcast_fusion.2
  125.0 6.8 convolution_bitcast_fusion.1
  138.2 16.1 %add.283 = f32[7,4,14,14,14,14]{5,4,3,2,1,0:T(8,128)} broadcast(f32[7,4,14,14,14]{4,3,2,1,0:T(8,128)} %copy.105), dimensions={0,1,2,3,5} | broadcast | bytes 4609920 | tf_op jit(solution)/shard_map/add | solution.py:92
  154.3 26.9 %add.284 = f32[7,4,196,196]{3,2,1,0:T(8,128)} reshape(f32[7,4,14,14,14,14]{5,4,3,2,1,0:T(8,128)} %add.283) | data formatting | bytes 8605184 | tf_op jit(solution)/shard_map/add | solution.py:92
  187.6 16.6 %add.280 = f32[7,4,14,14,14,14]{5,4,3,2,1,0:T(8,128)} broadcast(f32[7,4,14,14,14]{4,3,2,1,0:T(8,128)} %copy.101), dimensions={0,1,2,3,4} | broadcast | bytes 4609920 | tf_op jit(solution)/shard_map/add | solution.py:92
  204.2 26.9 %add.281 = f32[7,4,196,196]{3,2,1,0:T(8,128)} reshape(f32[7,4,14,14,14,14]{5,4,3,2,1,0:T(8,128)} %add.280) | data formatting | bytes 8605184 | tf_op jit(solution)/shard_map/add | solution.py:92
  231.0 6.9 copy.102
  267.0 35.7 %fusion = bf16[344,1280]{1,0:T(8,128)(2,1)} fusion(bf16[1372,1280]{1,0:T(8,128)(2,1)} %fusion.13), kind=kCustom, calls=%all-reduce-scatter | all-reduce-scatter fusion | flops 1761281 | bytes 4393472
  319.4 33.8 %all-gather.9.cloned.1.call-done = bf16[4,343,1280]{2,1,0:T(8,128)(2,1)} async-done(((bf16[1,343,1280]{2,1,0:T(8,128)(2,1)}), bf16[4,343,1280]{2,1,0:T(8,128)(2,1)}) %all-gather.9.cloned.1.call-update) | async-done | bytes 3512336 | tf_op jit(solution)/shard_map/all_gather | solution.py:284
  361.1 9.2 fusion.153
  370.3 15.8 %all-gather.7.cloned.1.call-done = bf16[4,343,1280]{2,1,0:T(8,128)(2,1)} async-done(((bf16[1,343,1280]{2,1,0:T(8,128)(2,1)}), bf16[4,343,1280]{2,1,0:T(8,128)(2,1)}) %all-gather.7.cloned.1.call-update) | async-done | bytes 3512336 | tf_op jit(solution)/shard_map/all_gather | solution.py:255
  398.9 22.5 %multiply_convert_fusion = (bf16[1372,1280]{1,0:T(8,128)(2,1)}, f32[1372,1280]{1,0:T(8,128)S(1)}, f32[1372,1280]{1,0:T(8,128)}) fusion(f32[1372,1280]{1,0:T(8,128)S(1)} %convolution_add_fusion, f32[1372,16]{0,1:T(8,128)S(1)} %fusion.80, bf16[8,16,1280]{2,1,0:T(8,128)(2,1)} %param.47, s32[]{:T(128)S(6)} %select_n.111), kind=kOutput, calls=%fused_computation.22 | convolution fusion | flops 454845440 | bytes 24715012 | tf_op jit(solution)/shard_map/dot_general | solution.py:36
  421.5 9.5 %add_convert_fusion = bf16[1372,1280]{1,0:T(8,128)(2,1)S(1)} fusion(f32[1372,1280]{1,0:T(8,128)S(1)} %get-tuple-element.31, f32[1372,1280]{1,0:T(8,128)S(1)} %bitcast.203, f32[1372,16]{0,1:T(8,128)S(1)} %fusion.70, f32[1372,1280]{1,0:T(8,128)} %get-tuple-element.47, bf16[8,1280,16]{1,2,0:T(8,128)(2,1)} %param.48, s32[]{:T(128)S(6)} %select_n.111), kind=kOutput, calls=%fused_computation.21 | convolution fusion | flops 365281280 | bytes 24735492 | tf_op jit(solution)/shard_map/dot_general | solution.py:36
  443.6 35.2 %fusion.2 = bf16[344,1280]{1,0:T(8,128)(2,1)} fusion(bf16[1372,1280]{1,0:T(8,128)(2,1)} %fusion.11), kind=kCustom, calls=%all-reduce-scatter.2 | all-reduce-scatter fusion | flops 1761281 | bytes 4393472
  481.8 6.7 concatenate.2
  521.2 9.3 all-gather.11.cloned.1.call-done
  601.1 26.1 %reshape.255 = f32[7,4,14,14,14,14]{5,4,3,2,1,0:T(8,128)} reshape(f32[7,4,196,196]{3,2,1,0:T(8,128)} %copy.117) | data formatting | bytes 8605184 | tf_op jit(solution)/shard_map/reshape | solution.py:127
  627.2 20.1 %fusion.145 = (f32[7,4,14,14,14]{4,3,2,1,0:T(8,128)}, f32[7,4,14,14,14]{4,3,2,1,0:T(8,128)}) fusion(f32[7,4,14,14,14,14]{5,4,3,2,1,0:T(8,128)} %reshape.255), kind=kLoop, calls=%fused_computation.240 | loop fusion | flops 1997632 | bytes 4917248 | tf_op jit(solution)/shard_map/reduce_sum | solution.py:129
  691.7 68.9 %fusion.146 = (bf16[344,1280]{1,0:T(8,128)(2,1)}, bf16[344,1280]{1,0:T(8,128)(2,1)}) fusion(bf16[1372,1280]{1,0:T(8,128)(2,1)} %fusion.12, bf16[1372,1280]{1,0:T(8,128)(2,1)} %fusion.10), kind=kCustom, calls=%all-reduce-scatter.4 | all-reduce-scatter fusion | flops 3522561 | bytes 8786432
  786.6 31.3 %all-reduce.14.cloned.1.call-done = (f32[8,1280,16]{1,2,0:T(8,128)}, f32[8,16,1280]{2,1,0:T(8,128)}, f32[8,1280,16]{1,2,0:T(8,128)}, f32[8,16,1280]{2,1,0:T(8,128)}) async-done(((f32[8,1280,16]{1,2,0:T(8,128)}, f32[8,16,1280]{2,1,0:T(8,128)}, f32[8,1280,16]{1,2,0:T(8,128)}, f32[8,16,1280]{2,1,0:T(8,128)}), (f32[8,1280,16]{1,2,0:T(8,128)}, f32[8,16,1280]{2,1,0:T(8,128)}, f32[8,1280,16]{1,2,0:T(8,128)}, ...) | async-done | bytes 2621456 | tf_op jit(solution)/shard_map/psum | solution.py:335
  817.8 107.7 %all-reduce.16.cloned.1.call-done = (f32[8,16,3,320]{3,1,2,0:T(8,128)}, f32[8,320,16]{1,2,0:T(8,128)}, f32[8,16,1280]{2,1,0:T(8,128)}, f32[8,1280,16]{1,2,0:T(8,128)}) async-done(((f32[8,16,3,320]{3,1,2,0:T(8,128)}, f32[8,320,16]{1,2,0:T(8,128)}, f32[8,16,1280]{2,1,0:T(8,128)}, f32[8,1280,16]{1,2,0:T(8,128)}), (f32[8,16,3,320]{3,1,2,0:T(8,128)}, f32[8,320,16]{1,2,0:T(8,128)}, f32[8,16,1280]{2,1,0:T(8,128)}, ...) | async-done | bytes 1966096 | tf_op jit(solution)/shard_map/psum | solution.py:326
  (308 shorter events, 354.0 us)
Async XLA Ops:
  7.2 386.8 %copy-start = (bf16[1280,1280]{1,0:T(8,128)(2,1)S(1)}, bf16[1280,1280]{1,0:T(8,128)(2,1)}, u32[]{:S(2)}) copy-start(bf16[1280,1280]{1,0:T(8,128)(2,1)} %param.38) | copy-start | bytes 9830404
  7.2 346.0 %all-gather.9.cloned.1.call-start = ((), (), s32[]{:S(2)}) async-start(), calls=%async_computation.1 | async-start | bytes 4403200 | tf_op jit(solution)/shard_map/all_gather | solution.py:284
  8.8 47.0 %copy-start.49 = (f32[343]{0:T(512)}, f32[343]{0:T(512)S(1)}, u32[]{:S(2)}) copy-start(f32[343]{0:T(512)S(1)} %broadcast_multiply_fusion.13) | copy-start | bytes 4120
  10.4 45.5 %copy-start.51 = (f32[343]{0:T(512)}, f32[343]{0:T(512)S(1)}, u32[]{:S(2)}) copy-start(f32[343]{0:T(512)S(1)} %add_rsqrt_fusion.1) | copy-start | bytes 4120
  11.1 44.8 %copy-start.47 = (f32[1280]{0:T(1024)}, f32[1280]{0:T(1024)S(1)}, u32[]{:S(2)}) copy-start(f32[1280]{0:T(1024)S(1)} %convert_element_type.157) | copy-start | bytes 15364
  13.6 13.2 %collective-permute-start = (bf16[343,1280]{1,0:T(8,128)(2,1)S(1)}, bf16[343,1280]{1,0:T(8,128)(2,1)}, u32[]{:S(2)}, u32[]{:S(2)}) collective-permute-start(bf16[343,1280]{1,0:T(8,128)(2,1)S(1)} %fusion.40), channel_id=1, source_target_pairs={{0,1},{1,2},{2,3},{3,0},{4,5},{5,6},{6,7},{7,4},{8,9},{9,10},{10,1... | collective-permute-start | bytes 2634248 | tf_op jit(solution)/shard_map/ppermute | solution.py:215
  26.9 12.7 %collective-permute-start.1 = (bf16[343,1280]{1,0:T(8,128)(2,1)}, bf16[343,1280]{1,0:T(8,128)(2,1)}, u32[]{:S(2)}, u32[]{:S(2)}) collective-permute-start(bf16[343,1280]{1,0:T(8,128)(2,1)} %collective-permute-done), channel_id=1, source_target_pairs={{0,1},{1,2},{2,3},{3,0},{4,5},{5,6},{6,7},{7,4},{8,9},{9,10},{10,1... | collective-permute-start | bytes 2634248 | tf_op jit(solution)/shard_map/ppermute | solution.py:215
  30.5 43.5 %copy-start.45 = (bf16[16,960]{1,0:T(8,128)(2,1)}, bf16[16,960]{1,0:T(8,128)(2,1)S(1)}, u32[]{:S(2)}) copy-start(bf16[16,960]{1,0:T(8,128)(2,1)S(1)} %reshape.242) | copy-start | bytes 92164
  31.0 94.1 %copy-start.40 = (bf16[14,14,80,1,1]{2,1,0,3,4:T(8,128)(2,1)}, bf16[14,14,80,1,1]{2,1,0,3,4:T(8,128)(2,1)S(1)}, u32[]{:S(2)}) copy-start(bf16[14,14,80,1,1]{2,1,0,3,4:T(8,128)(2,1)S(1)} %reshape.271) | copy-start | bytes 94084
  39.6 12.7 %collective-permute-start.2 = (bf16[343,1280]{1,0:T(8,128)(2,1)}, bf16[343,1280]{1,0:T(8,128)(2,1)}, u32[]{:S(2)}, u32[]{:S(2)}) collective-permute-start(bf16[343,1280]{1,0:T(8,128)(2,1)} %collective-permute-done.1), channel_id=1, source_target_pairs={{0,1},{1,2},{2,3},{3,0},{4,5},{5,6},{6,7},{7,4},{8,9},{9,10},{10,1... | collective-permute-start | bytes 2634248 | tf_op jit(solution)/shard_map/ppermute | solution.py:215
  40.0 72.4 %copy-start.42 = (bf16[14,14,80,1,1]{2,1,0,3,4:T(8,128)(2,1)}, bf16[14,14,80,1,1]{2,1,0,3,4:T(8,128)(2,1)S(1)}, u32[]{:S(2)}) copy-start(bf16[14,14,80,1,1]{2,1,0,3,4:T(8,128)(2,1)S(1)} %reshape.270) | copy-start | bytes 94084
  267.0 37.8 %copy-start.54 = (bf16[1280]{0:T(1024)(128)(2,1)S(1)}, bf16[1280]{0:T(1024)(128)(2,1)}, u32[]{:S(2)}) copy-start(bf16[1280]{0:T(1024)(128)(2,1)} %param.36) | copy-start | bytes 7684
  267.0 37.8 %copy-start.55 = (bf16[1280]{0:T(1024)(128)(2,1)S(1)}, bf16[1280]{0:T(1024)(128)(2,1)}, u32[]{:S(2)}) copy-start(bf16[1280]{0:T(1024)(128)(2,1)} %param.37) | copy-start | bytes 7684
  267.0 37.8 %copy-start.59 = (u32[32]{0:T(128)S(1)}, u32[32]{0:T(128)}, u32[]{:S(2)}) copy-start(u32[32]{0:T(128)} %constant.219) | copy-start | bytes 388
  303.5 2.6 collective-permute-start.3
  318.6 67.4 %all-gather.7.cloned.1.call-start = ((), (), s32[]{:S(2)}) async-start(), calls=%async_computation | async-start | bytes 4403200 | tf_op jit(solution)/shard_map/all_gather | solution.py:255
  319.4 211.2 %all-gather.11.cloned.1.call-start = ((), (), s32[]{:S(2)}) async-start(), calls=%async_computation.2 | async-start | bytes 4403200 | tf_op jit(solution)/shard_map/all_gather | solution.py:302
  361.1 60.4 %copy-start.37 = (f32[1372,16]{0,1:T(8,128)}, f32[1372,16]{0,1:T(8,128)S(1)}, u32[]{:S(2)}) copy-start(f32[1372,16]{0,1:T(8,128)S(1)} %fusion.70) | copy-start | bytes 263428
  479.5 2.2 collective-permute-start.5
  495.8 322.0 %all-reduce.14.cloned.1.call-start = ((), (), s32[]{:S(2)}) async-start(), calls=%async_computation.3 | async-start | bytes 5242880 | tf_op jit(solution)/shard_map/psum | solution.py:335
  679.3 246.2 %all-reduce.16.cloned.1.call-start = ((), (), s32[]{:S(2)}) async-start(), calls=%async_computation.4 | async-start | bytes 4194304 | tf_op jit(solution)/shard_map/psum | solution.py:326
  691.6 74.8 %copy-start.57 = (bf16[1280]{0:T(1024)(128)(2,1)S(1)}, bf16[1280]{0:T(1024)(128)(2,1)}, u32[]{:S(2)}) copy-start(bf16[1280]{0:T(1024)(128)(2,1)} %param.41) | copy-start | bytes 7684
  761.3 5.2 collective-permute-start.6
  763.3 9.2 collective-permute-start.4
  (56 other events, 454.7 us)
Sparse Core Ops, SparseCore 0:
  318.7 34.4 all-gather.8
  355.4 30.6 all-gather.6
  495.9 34.5 all-gather.10
  679.4 138.3 all-reduce.13
  823.3 102.1 all-reduce.15
